TPU v7x, 512 devices: a whole 4x8x8 slice. The times are simulated.
512 devices in a mesh: ctx: 128 (over x, z_hi, y, core), kvh: 4 (over z_lo).
Axes of the slice: x: 4, y: 8, z: 8 (z_hi: 2, z_lo: 4; z = z_hi * 4 + z_lo), core: 2. Of those that a mesh axis runs over, the one named last changes fastest.
Arguments:
- queries: bfloat16 [16384, 2048], P('ctx', 'kvh'), parts along dimension 1, may hold values from -56 to 56
- keys: bfloat16 [16384, 512], P('ctx', 'kvh'), parts along dimension 1, may hold values from -4 to 4
- values: bfloat16 [16384, 512], P('ctx', 'kvh'), parts along dimension 1, may hold values from -6 to 6
- segment_ids: int32 [16384], P('ctx'), may hold values from 0 to 15, never falling along the last dimension, each value on 1 to 8320 neighbouring positions
Outputs:
- attended: bfloat16 [16384, 2048], P('ctx', 'kvh'), parts along dimension 1
There are 4 independent parts, one for each index of `kvh`. A program takes and returns all parts, laid end to end along the dimension named above; an argument that names none is the same for every part. Nothing has to cross between parts.
All inputs are finite; a program needn't handle non-finite values.
Results may differ from a plain program's by a relative error of at most 0.0045.
Values may be sent and summed in bfloat16 or wider, within the bound.
A program may use at most 128 MiB of HBM per device.

v0:
```python
import jax
import jax.numpy as jnp
from jax import lax
from jax.sharding import PartitionSpec as P


def fold_step(carry, piece, start, query_heads, query_pos, query_seg):
    key_rows, value_rows, key_seg = piece
    count = key_rows.shape[0]
    scale = key_rows.shape[1] ** (-0.5)

    def attend(state):
        running, total, summed = state
        score = (
            jnp.einsum("thd,nd->thn", query_heads, key_rows, preferred_element_type=jnp.float32)
            * scale
        )
        key_pos = jnp.arange(count, dtype=jnp.int32)
        allowed = (
            (key_pos[None, :] <= query_pos[:, None])
            & (key_pos[None, :] >= 0)
            & (key_seg[None, :] == query_seg[:, None])
        )
        masked = jnp.where(allowed[:, None, :], score, -1e30)
        new_top = jnp.maximum(running, jnp.max(masked, axis=2))
        weight = jnp.where(allowed[:, None, :], jnp.exp(masked - new_top[:, :, None]), 0.0)
        new_total = jnp.sum(weight, axis=2)
        product = jnp.einsum(
            "thn,nd->thd",
            weight.astype(jnp.bfloat16),
            value_rows,
            preferred_element_type=jnp.float32,
        )
        return (new_top, new_total, product)

    live = start <= jnp.max(query_pos)
    return lax.cond(live, attend, lambda state: state, carry)


def empty_state(rows, heads, head_dim):
    return (
        jnp.full((rows, heads), -1e30, jnp.float32),
        jnp.zeros((rows, heads), jnp.float32),
        jnp.zeros((rows, heads, head_dim), jnp.float32),
    )


def finish(state):
    running, total, summed = state
    rows, heads, head_dim = summed.shape
    return (summed / total[:, :, None]).reshape(rows, heads * head_dim).astype(jnp.bfloat16)


def body(queries, keys, values, segment_ids):
    tok_rows = queries.shape[0]
    head_dim = keys.shape[1]
    heads = queries.shape[1] // head_dim
    mine = lax.axis_index("ctx")
    query_heads = queries.reshape(tok_rows, heads, head_dim)
    query_pos = mine * tok_rows + jnp.arange(tok_rows, dtype=jnp.int32)
    state = fold_step(
        empty_state(tok_rows, heads, head_dim),
        (
            lax.all_gather(keys, "ctx", axis=0, tiled=True),
            lax.all_gather(values, "ctx", axis=0, tiled=True),
            lax.all_gather(segment_ids, "ctx", axis=0, tiled=True),
        ),
        jnp.int32(0),
        query_heads,
        query_pos,
        segment_ids,
    )
    return finish(state)


def solution(mesh):
    return jax.shard_map(
        body,
        mesh=mesh,
        in_specs=(P("ctx", "kvh"), P("ctx", "kvh"), P("ctx", "kvh"), P("ctx")),
        out_specs=P("ctx", "kvh"),
        check_vma=False,
    )
```

profile of v0, /device:TPU:7, one launch (start us, length us, event | category | flops | bytes accessed | tf_op | source)
XLA Modules:
  0.0 353.8 jit_solution(3457269656546954463)
XLA Ops:
  6.5 0.0 all-gather.4.cloned.1.call-start
  6.5 0.7 all-gather.4.cloned.1.call-update
  7.3 0.0 all-gather.6.cloned.1.call-start
  7.3 0.7 all-gather.6.cloned.1.call-update
  8.0 0.6 fusion.16
  9.3 206.3 %all-gather = s32[128,1,128]{2,1,0:T(1,128)S(1)} all-gather(s32[1,1,128]{2,1,0:T(1,128)} %bitcast.25), channel_id=1, replica_groups=mesh['ctx'=128,'kvh'=4] {'ctx'}, dimensions={0}, use_global_device_ids=true | all-gather | bytes 66048 | tf_op jit(solution)/shard_map/all_gather | solution.py:66
  215.6 0.0 all-gather.4.cloned.1.call-done
  215.6 78.9 %all-gather.6.cloned.1.call-done = bf16[16384,128]{1,0:T(8,128)(2,1)} async-done(((bf16[128,128]{1,0:T(8,128)(2,1)}), bf16[16384,128]{1,0:T(8,128)(2,1)}) %all-gather.6.cloned.1.call-update) | async-done | bytes 4194320 | tf_op jit(solution)/shard_map/all_gather | solution.py:65
  294.4 51.8 %conditional.1 = (f32[128,4]{0,1:T(4,128)S(1)}, f32[128,4,128]{2,0,1:T(8,128)S(1)}) conditional(s32[]{:T(128)} %convert_element_type.12, () %tuple.13, (s32[128]{0:T(128)S(1)}, s32[16384]{0:T(1024)S(1)}, s32[128]{0:T(128)}, bf16[128,512]{1,0:T(8,128)(2,1)}, bf16[16384,128]{1,0:T(8,128)(2,1)}, /*index=5*/bf16[16384,128]{1,0:T(8,128)(2,1)}) %tuple.22), branch_computations={%region_1.0_spmd, %region_2.5_spmd} | conditional | flops 4410310144 | bytes 117912592 | solution.py:37
  294.4 2.4 fusion.6
  296.8 15.5 %fusion = (f32[128,4]{0,1:T(4,128)S(1)}, f32[128,4,16384]{2,0,1:T(8,128)}) fusion(pred[128,16384]{1,0:T(8,128)(4,1)S(1)} %fusion.6, bf16[16384,128]{1,0:T(8,128)(2,1)} %get-tuple-element.22, bf16[128,512]{1,0:T(8,128)(2,1)} %get-tuple-element.29), kind=kOutput, calls=%fused_computation.2 | convolution fusion | flops 2172648960 | bytes 39979008 | tf_op jit(solution)/shard_map/cond/branch_1_fun/thd,nd->thn/dot_general | solution.py:15
  312.3 18.3 %fusion.3 = f32[128,4,128]{2,0,1:T(8,128)S(1)} fusion(f32[128,4,16384]{2,0,1:T(8,128)} %get-tuple-element.31, f32[128,4]{0,1:T(4,128)S(1)} %broadcast_maximum_fusion, pred[128,16384]{1,0:T(8,128)(4,1)S(1)} %fusion.6, bf16[16384,128]{1,0:T(8,128)(2,1)} %get-tuple-element.23), kind=kOutput, calls=%fused_computation.5 | convolution fusion | flops 2189426688 | bytes 40110080 | tf_op jit(solution)/shard_map/cond/branch_1_fun/thn,nd->thd/dot_general | solution.py:28
  330.6 15.6 %fusion.2 = f32[128,4]{0,1:T(4,128)S(1)} fusion(f32[128,4,16384]{2,0,1:T(8,128)} %get-tuple-element.31, f32[128,4]{0,1:T(4,128)S(1)} %broadcast_maximum_fusion, pred[128,16384]{1,0:T(8,128)(4,1)S(1)} %fusion.6), kind=kLoop, calls=%fused_computation.4 | loop fusion | flops 41942528 | bytes 35655680 | tf_op jit(solution)/shard_map/cond/branch_1_fun/reduce_sum | solution.py:27
  346.2 0.8 copy_bitcast_fusion
  (2 shorter events, 0.0 us)
Async XLA Ops:
  6.5 209.0 %all-gather.4.cloned.1.call-start = ((), (), s32[]{:S(2)}) async-start(), calls=%async_computation | async-start | bytes 4227072 | tf_op jit(solution)/shard_map/all_gather | solution.py:64
  7.3 287.2 %all-gather.6.cloned.1.call-start = ((), (), s32[]{:S(2)}) async-start(), calls=%async_computation.1 | async-start | bytes 4227072 | tf_op jit(solution)/shard_map/all_gather | solution.py:65
Sparse Core Ops, SparseCore 0:
  11.9 144.7 all-gather.3
  161.3 133.0 all-gather.5
where the time goes:
time: 355 us; the launch traced here: 354 us
  blocking collectives  206 us (58%)
  waiting for transfers between devices  80.3 us (23%)
  matrix products  33.8 us (10%)
  other arithmetic  19.4 us (5%)
  between operations  14.1 us (4%)
    all_gather x1, blocking collectives, body(): lax.all_gather(segment_ids, 'ctx', axis=0, tiled=True)  206 us
    all_gather x1, waiting for transfers between devices, body(): lax.all_gather(values, 'ctx', axis=0, tiled=True)  78.9 us
    dot_general x1, matrix products, attend(): jnp.einsum('thn,nd->thd', weight.astype(jnp.bfloat16), value_rows, prefer...  18.3 us
    reduce_sum x1, other arithmetic, attend(): new_total = jnp.sum(weight, axis=2)  15.6 us
    dot_general x1, matrix products, attend(): jnp.einsum('thd,nd->thn', query_heads, key_rows, preferred_element_type=j...  15.5 us
  transfers between devices with their start and end apart: 2, of which 1 were waited for; matrix products, arithmetic and copies ran while one was open for 0% of the time, Pallas kernels for 0%

commit v1 on v0

v1 whole, which is shorter than its diff:
```python
import functools
import math

import jax
import jax.numpy as jnp
from jax import lax
from jax.experimental import pallas as pl
from jax.experimental.pallas import tpu as pltpu
from jax.sharding import PartitionSpec as P

MESH = pl.DeviceIdType.MESH
RING = 8
BLOCKS = 2 * RING
RINGS = 8
REACH = 4
TOK = 128
HEAD = 128
HEADS = 4
ROWS = 272
LOW = -2e30
ITEMS = REACH + 1


def kernel(
    q_ref, k_ref, v_ref, seg_ref, o_ref,
    kv, edge, qseg, top, total, summed,
    xz_send, xz_recv, y_send, y_recv, c_send, c_recv, e_send, e_recv,
):
    me = lax.axis_index("ctx")
    off = lax.rem(me, BLOCKS)
    ring = me // BLOCKS
    c = lax.rem(me, 2)
    y = off // 2
    unit_scale = HEAD**-0.5 * math.log2(math.e)

    def at(dy):
        return 2 * lax.rem(y + dy + RING, RING) + c

    up = ring * BLOCKS + at(1)
    down = ring * BLOCKS + at(-1)
    twin = me + 1 - 2 * c

    def remote(src, dst, send, recv, to):
        return pltpu.make_async_remote_copy(
            src_ref=src, dst_ref=dst, send_sem=send, recv_sem=recv,
            device_id={"ctx": to}, device_id_type=MESH,
        )

    has_edge = (off == 0) & (ring >= ITEMS)
    gives_edge = (off == BLOCKS - 1) & (ring + ITEMS < RINGS)

    barrier = pltpu.get_barrier_semaphore()
    for to in (up, down, twin):
        pl.semaphore_signal(barrier, inc=1, device_id={"ctx": to}, device_id_type=MESH)
    for d in range(1, ITEMS):

        @pl.when(ring >= d)
        def _():
            pl.semaphore_signal(
                barrier, inc=1, device_id={"ctx": me - d * BLOCKS}, device_id_type=MESH
            )

    @pl.when(has_edge)
    def _():
        pl.semaphore_signal(
            barrier, inc=1, device_id={"ctx": me - REACH * BLOCKS - 1}, device_id_type=MESH
        )

    kv[0, off, pl.ds(0, TOK), :] = k_ref[...]
    kv[0, off, pl.ds(TOK, TOK), :] = v_ref[...]
    seg_row = seg_ref[...].astype(jnp.float32)
    kv[0, off, pl.ds(2 * TOK, 16), :] = jnp.broadcast_to(seg_row, (16, TOK)).astype(jnp.bfloat16)
    qseg[...] = jnp.broadcast_to(seg_row, (TOK, TOK)).T
    top[...] = jnp.full(top.shape, -1e30, jnp.float32)
    total[...] = jnp.zeros_like(total)
    summed[...] = jnp.zeros_like(summed)

    pl.semaphore_wait(
        barrier, 3 + jnp.minimum(RINGS - 1 - ring, REACH) + gives_edge.astype(jnp.int32)
    )

    def delta(k):
        return lax.rem(2 * k, ITEMS)

    def xz(k, to):
        return remote(
            kv.at[0, off], kv.at[k, off], xz_send.at[k], xz_recv.at[k], to
        )

    def hop(k, dy, slot, to):
        b = at(dy)
        return remote(kv.at[k, b], kv.at[k, b], y_send.at[k, slot], y_recv.at[k, slot], to)

    def cross(k, dy, slot):
        b = at(dy)
        return remote(kv.at[k, b], kv.at[k, b], c_send.at[k, slot], c_recv.at[k, slot], twin)

    def cross_in(k, dy, slot):
        b = 2 * lax.rem(y + dy + RING, RING) + 1 - c
        return remote(kv.at[k, b], kv.at[k, b], c_send.at[k, slot], c_recv.at[k, slot], twin)

    def launch(k):
        hop(k, 0, 1, up).start()
        hop(k, 0, 4, down).start()
        cross(k, 0, 0).start()

    launch(0)
    for k in (3, 4, 1, 2):
        d = 2 * k % ITEMS

        @pl.when(ring + d < RINGS)
        def _():
            xz(k, me + d * BLOCKS).start()

    def edge_copy(to):
        return remote(kv.at[0, off], edge, e_send, e_recv, to)

    @pl.when(gives_edge)
    def _():
        edge_copy(me + REACH * BLOCKS + 1).start()

    def arrive(k, h):
        if h < 4:
            hop(k, -h, h, up).wait_recv()
            if h < 3:
                hop(k, -h, h + 1, up).start()
            else:

                @pl.when(c == 0)
                def _():
                    hop(k, -3, 7, up).start()

            cross(k, -h, h).start()
            hop(k, h, 3 + h, down).wait_recv()
            if h < 3:
                hop(k, h, 4 + h, down).start()
            else:

                @pl.when(c == 1)
                def _():
                    hop(k, 3, 7, down).start()

            cross(k, h, 3 + h).start()
        else:
            hop(k, 4, 7, up).wait_recv()
            cross(k, 4, 7).start()

    lane = lax.broadcasted_iota(jnp.int32, (TOK, TOK), 1)
    row = lax.broadcasted_iota(jnp.int32, (TOK, TOK), 0)
    gap = row - lane

    def fold(blocks, ahead):
        keys = jnp.concatenate([b[pl.ds(0, TOK), :] for b in blocks], axis=0)
        values = jnp.concatenate([b[pl.ds(TOK, TOK), :] for b in blocks], axis=0)
        allowed = []
        for b, a in zip(blocks, ahead):
            seg = b[pl.ds(2 * TOK, 16), :].astype(jnp.float32)[0:1, :]
            allowed.append((seg == qseg[...]) & (gap >= a))
        for h in range(HEADS):
            score = lax.dot_general(
                q_ref[:, h * HEAD : (h + 1) * HEAD], keys, (((1,), (1,)), ((), ())),
                preferred_element_type=jnp.float32,
            )
            parts = [
                jnp.where(allowed[n], score[:, n * TOK : (n + 1) * TOK] * unit_scale, LOW)
                for n in range(len(blocks))
            ]
            old = top[h]
            most = functools.reduce(jnp.maximum, parts)
            new = jnp.maximum(old, jnp.max(most, axis=1, keepdims=True))
            keep = jnp.exp2(old - new)
            weights = [jnp.exp2(p - new) for p in parts]
            top[h] = new
            total[h] = total[h] * keep + functools.reduce(jnp.add, weights)
            rounded = jnp.concatenate([w.astype(jnp.bfloat16) for w in weights], axis=1)
            summed[h] = summed[h] * keep + jnp.dot(
                rounded, values, preferred_element_type=jnp.float32
            )

    def unit(k, h):
        if h < 4:
            cross_in(k, -h, h).wait_recv()
            cross_in(k, h, 3 + h).wait_recv()
            first = (-h, h)
        else:
            cross_in(k, 0, 0).wait_recv()
            cross_in(k, 4, 7).wait_recv()
            first = (0, 4)
        blocks, ahead = [], []
        for dy in first:
            chip = lax.rem(y + dy + RING, RING)
            for core in range(2):
                b = 2 * chip + core
                blocks.append(kv.at[k, b])
                ahead.append((b - off - delta(k) * BLOCKS) * TOK)
        fold(blocks, ahead)

    def drain(k):
        for slot in range(1, 7):
            hop(k, 0, slot, up).wait_send()
        hop(k, 0, 7, up).wait_send()
        for slot in range(8):
            cross(k, 0, slot).wait_send()

    def here(k):
        return (k >= 0) & (k < ITEMS) & (ring >= delta(jnp.maximum(k, 0)))

    def step(j, _):
        @pl.when(here(j - 1))
        def _():
            arrive(j - 1, 3)

        @pl.when(here(j))
        def _():
            arrive(j, 1)

        @pl.when(here(j - 2))
        def _():
            unit(j - 2, 4)

        @pl.when(here(j - 1))
        def _():
            unit(j - 1, 2)

        @pl.when(here(j - 1))
        def _():
            arrive(j - 1, 4)

        @pl.when(here(j))
        def _():
            arrive(j, 2)

        @pl.when(here(j + 1))
        def _():
            xz(j + 1, me).wait_recv()
            launch(j + 1)

        @pl.when(here(j - 1))
        def _():
            unit(j - 1, 3)

        @pl.when(here(j))
        def _():
            unit(j, 1)

        @pl.when(here(j - 2))
        def _():
            drain(j - 2)

        @pl.when(has_edge & (j == 4))
        def _():
            edge_copy(me).wait_recv()
            fold([edge], [jnp.int32(-ITEMS * BLOCKS * TOK + (BLOCKS - 1) * TOK)])

        return 0

    lax.fori_loop(0, ITEMS + 2, step, 0)

    for h in range(HEADS):
        whole = jnp.sum(total[h], axis=1, keepdims=True)
        o_ref[:, h * HEAD : (h + 1) * HEAD] = (summed[h] / whole).astype(jnp.bfloat16)

    for k in range(1, ITEMS):
        d = 2 * k % ITEMS

        @pl.when(ring + d < RINGS)
        def _():
            xz(k, me).wait_send()

    @pl.when(gives_edge)
    def _():
        edge_copy(me).wait_send()


def body(queries, keys, values, segment_ids):
    vmem = pl.BlockSpec(memory_space=pltpu.VMEM)
    return pl.pallas_call(
        kernel,
        out_shape=jax.ShapeDtypeStruct(queries.shape, queries.dtype),
        in_specs=[vmem] * 4,
        out_specs=vmem,
        scratch_shapes=[
            pltpu.VMEM((ITEMS, BLOCKS, ROWS, HEAD), jnp.bfloat16),
            pltpu.VMEM((ROWS, HEAD), jnp.bfloat16),
            pltpu.VMEM((TOK, TOK), jnp.float32),
            pltpu.VMEM((HEADS, TOK, HEAD), jnp.float32),
            pltpu.VMEM((HEADS, TOK, HEAD), jnp.float32),
            pltpu.VMEM((HEADS, TOK, HEAD), jnp.float32),
            pltpu.SemaphoreType.DMA((ITEMS,)),
            pltpu.SemaphoreType.DMA((ITEMS,)),
            pltpu.SemaphoreType.DMA((ITEMS, 8)),
            pltpu.SemaphoreType.DMA((ITEMS, 8)),
            pltpu.SemaphoreType.DMA((ITEMS, 8)),
            pltpu.SemaphoreType.DMA((ITEMS, 8)),
            pltpu.SemaphoreType.DMA,
            pltpu.SemaphoreType.DMA,
        ],
        compiler_params=pltpu.CompilerParams(
            collective_id=0, has_side_effects=True, vmem_limit_bytes=40 << 20
        ),
        name="attend_ring",
    )(queries, keys, values, segment_ids.reshape(1, TOK))


def solution(mesh):
    return jax.shard_map(
        body,
        mesh=mesh,
        in_specs=(P("ctx", "kvh"), P("ctx", "kvh"), P("ctx", "kvh"), P("ctx")),
        out_specs=P("ctx", "kvh"),
        check_vma=False,
    )
```

time: 355 us -> 69.8 us (0.20)
  blocking collectives: 206 us -> 0 us
  waiting for transfers between devices: 80.3 us -> 0 us
  Pallas kernels: 0 us -> 65.1 us
  matrix products: 33.8 us -> 0 us
  other arithmetic: 19.4 us -> 0 us
  between operations: 14.1 us -> 0.01 us
  local copies, waits for them, and re-layouts: 0 us -> 3.73 us
    all_gather x1 -> x0, blocking collectives: 206 us -> none  [body(): lax.all_gather(segment_ids, 'ctx', axis=0, tiled=True)]
    all_gather x2 -> x0, waiting for transfers between devices: 78.9 us -> none  [the longest x1 78.9 us: body(): lax.all_gather(values, 'ctx', axis=0, tiled=True)]
    pallas_call x0 -> x1, Pallas kernels: none -> 65.1 us  [body(): pl.pallas_call(kernel, out_shape=jax.ShapeDtypeStruct(queries.shape, quer...]
    dot_general x2 -> x0, matrix products: 33.8 us -> none  [the longest x1 18.3 us: attend(): jnp.einsum('thn,nd->thd', weight.astype(jnp.bfloat16), value_rows, prefer...]
    reduce_sum x1 -> x0, other arithmetic: 15.6 us -> none  [attend(): new_total = jnp.sum(weight, axis=2)]
    unnamed x0 -> x9, local copies, waits for them, and re-layouts: none -> 3.73 us
  transfers between devices with their start and end apart: 2 -> 0, of which waited for: 1 -> 0; matrix products, arithmetic and copies ran while one was open for 0% -> 0% of each run, Pallas kernels for 0% -> 0%
where the time goes in v1:
time: 69.8 us; the launch traced here: 68.8 us
  Pallas kernels  65.1 us (93%)
  local copies, waits for them, and re-layouts  3.73 us (5%)
    pallas_call x1, Pallas kernels, body(): pl.pallas_call(kernel, out_shape=jax.ShapeDtypeStruct(queries.shape, quer...  65.1 us
    unnamed x9, local copies, waits for them, and re-layouts  3.73 us

profile of v1, /device:TPU:7, one launch (start us, length us, event | category | flops | bytes accessed | tf_op | source)
XLA Modules:
  0.0 68.8 jit_solution(9279609824573400460)
XLA Ops:
  0.0 0.0 copy-start.3
  0.0 0.7 copy-done.3
  0.7 0.0 copy-start
  0.7 0.9 %copy-done = bf16[128,512]{1,0:T(8,128)(2,1)S(1)} copy-done((bf16[128,512]{1,0:T(8,128)(2,1)S(1)}, bf16[128,512]{1,0:T(8,128)(2,1)}, u32[]{:S(2)}) %copy-start) | copy-done | bytes 131096
  1.6 0.0 copy-start.1
  1.6 0.8 %copy-done.1 = bf16[128,128]{1,0:T(8,128)(2,1)S(1)} copy-done((bf16[128,128]{1,0:T(8,128)(2,1)S(1)}, bf16[128,128]{1,0:T(8,128)(2,1)}, u32[]{:S(2)}) %copy-start.1) | copy-done | bytes 32792
  2.3 0.0 copy-start.2
  2.3 0.8 %copy-done.2 = bf16[128,128]{1,0:T(8,128)(2,1)S(1)} copy-done((bf16[128,128]{1,0:T(8,128)(2,1)S(1)}, bf16[128,128]{1,0:T(8,128)(2,1)}, u32[]{:S(2)}) %copy-start.2) | copy-done | bytes 32792
  3.1 65.1 %attend_ring.1 = bf16[128,512]{1,0:T(8,128)(2,1)S(1)} custom-call(bf16[128,512]{1,0:T(8,128)(2,1)S(1)} %copy-done, bf16[128,128]{1,0:T(8,128)(2,1)S(1)} %copy-done.1, bf16[128,128]{1,0:T(8,128)(2,1)S(1)} %copy-done.2, s32[1,128]{1,0:T(1,128)S(1)} %bitcast.1), custom_call_target="tpu_custom_call" | custom-call | tf_op jit(solution)/shard_map/attend_ring/pallas_call | solution.py:277
  68.2 0.7 copy.6
Async XLA Ops:
  0.0 0.7 copy-start.3
  0.7 0.9 %copy-start = (bf16[128,512]{1,0:T(8,128)(2,1)S(1)}, bf16[128,512]{1,0:T(8,128)(2,1)}, u32[]{:S(2)}) copy-start(bf16[128,512]{1,0:T(8,128)(2,1)} %q_ref.1) | copy-start | bytes 393220
  1.6 0.8 %copy-start.1 = (bf16[128,128]{1,0:T(8,128)(2,1)S(1)}, bf16[128,128]{1,0:T(8,128)(2,1)}, u32[]{:S(2)}) copy-start(bf16[128,128]{1,0:T(8,128)(2,1)} %k_ref.1) | copy-start | bytes 98308
  2.3 0.8 %copy-start.2 = (bf16[128,128]{1,0:T(8,128)(2,1)S(1)}, bf16[128,128]{1,0:T(8,128)(2,1)}, u32[]{:S(2)}) copy-start(bf16[128,128]{1,0:T(8,128)(2,1)} %v_ref.1) | copy-start | bytes 98308

commit v2 on v1

v2 whole, which is shorter than its diff:
```python
import functools
import math

import jax
import jax.numpy as jnp
from jax import lax
from jax.experimental import pallas as pl
from jax.experimental.pallas import tpu as pltpu
from jax.sharding import PartitionSpec as P

MESH = pl.DeviceIdType.MESH
RING = 8
BLOCKS = 2 * RING
RINGS = 8
REACH = 4
TOK = 128
HEAD = 128
HEADS = 4
ROWS = 272
LOW = -2e30
ITEMS = REACH + 1
LAG = 2
BACK = (0, 2, 4, 1, 3)
MEET_LO = 3
WAIT_LO, WAIT_HI = 5, 4
X_LAG = 3


def kernel(
    q_ref, k_ref, v_ref, seg_ref, o_ref,
    q, segs, kv, edge, qseg, top, total, summed, in_sem,
    xz_send, xz_recv, y_send, y_recv, x_send, x_recv, c_send, c_recv, e_send, e_recv,
):
    me = lax.axis_index("ctx")
    off = lax.rem(me, BLOCKS)
    ring = me // BLOCKS
    c = lax.rem(me, 2)
    y = off // 2
    unit_scale = HEAD**-0.5 * math.log2(math.e)

    def at(dy):
        return 2 * lax.rem(y + dy + RING, RING) + c

    up = ring * BLOCKS + at(1)
    down = ring * BLOCKS + at(-1)
    twin = me + 1 - 2 * c

    def remote(src, dst, send, recv, to):
        return pltpu.make_async_remote_copy(
            src_ref=src, dst_ref=dst, send_sem=send, recv_sem=recv,
            device_id={"ctx": to}, device_id_type=MESH,
        )

    half = lax.rem(ring, 2)

    loads = [
        pltpu.make_async_copy(seg_ref, segs, in_sem.at[0]),
        pltpu.make_async_copy(k_ref, kv.at[0, off, pl.ds(0, TOK)], in_sem.at[1]),
        pltpu.make_async_copy(v_ref, kv.at[0, off, pl.ds(TOK, TOK)], in_sem.at[2]),
    ] + [
        pltpu.make_async_copy(
            q_ref.at[:, pl.ds(h * HEAD, HEAD)], q.at[pl.ds(h * TOK, TOK)], in_sem.at[3 + h]
        )
        for h in range(HEADS)
    ]
    for load in loads:
        load.start()

    has_edge = (off == 0) & (ring >= ITEMS)
    gives_edge = (off == BLOCKS - 1) & (ring + ITEMS < RINGS)

    barrier = pltpu.get_barrier_semaphore()

    def greet(to):
        pl.semaphore_signal(barrier, inc=1, device_id={"ctx": to}, device_id_type=MESH)

    def greet_half():
        @pl.when(ring >= 1)
        def _():
            greet(me - BLOCKS)

        @pl.when(ring + 1 < RINGS)
        def _():
            greet(me + BLOCKS)

        @pl.when(has_edge)
        def _():
            greet(me - REACH * BLOCKS - 1)

        @pl.when(gives_edge)
        def _():
            greet(me + REACH * BLOCKS + 1)

    def one(x):
        return x.astype(jnp.int32)

    others = one(ring >= 1) + one(ring + 1 < RINGS) + one(has_edge) + one(gives_edge)

    for to in (up, down, twin):
        greet(to)
    for d in (2, 4):

        @pl.when(ring >= d)
        def _():
            greet(me - d * BLOCKS)

    top[...] = jnp.full(top.shape, -1e30, jnp.float32)
    total[...] = jnp.zeros_like(total)
    summed[...] = jnp.zeros_like(summed)
    loads[0].wait()
    seg_row = segs[...].astype(jnp.float32)
    kv[0, off, pl.ds(2 * TOK, 16), :] = jnp.broadcast_to(seg_row, (16, TOK)).astype(jnp.bfloat16)
    qseg[...] = jnp.broadcast_to(seg_row, (TOK, TOK)).T
    for load in loads[1:]:
        load.wait()

    pl.semaphore_wait(
        barrier, 3 + one(ring + 2 < RINGS) + one(ring + 4 < RINGS) + half * others
    )
    greet_half()

    def delta(k):
        return lax.rem(2 * k, ITEMS)

    def xz(k, to):
        return remote(kv.at[0, off], kv.at[k, off], xz_send.at[k], xz_recv.at[k], to)

    def hop(k, dy, slot, to):
        b = at(dy)
        return remote(kv.at[k, b], kv.at[k, b], y_send.at[k, slot], y_recv.at[k, slot], to)

    def along(k, dy, slot):
        b = at(dy)
        return remote(
            kv.at[k, b], kv.at[k + 1, b], x_send.at[k, slot], x_recv.at[k + 1, slot],
            me + 2 * BLOCKS,
        )

    def cross(k, dy, slot):
        b = at(dy)
        return remote(kv.at[k, b], kv.at[k, b], c_send.at[k, slot], c_recv.at[k, slot], twin)

    def cross_in(k, dy, slot):
        b = 2 * lax.rem(y + dy + RING, RING) + 1 - c
        return remote(kv.at[k, b], kv.at[k, b], c_send.at[k, slot], c_recv.at[k, slot], twin)

    def from_x(k):
        return (k == 1) | (k == 4)

    def feeds_x(k):
        return ((k == 0) | (k == 3)) & (ring + 2 < RINGS)

    def pass_on(k, dy, slot):
        @pl.when(feeds_x(k))
        def _():
            along(k, dy, slot).start()

        cross(k, dy, slot).start()

    def x_in(k, slot):
        return remote(
            kv.at[k - 1, off], kv.at[k, off], x_send.at[k - 1, slot], x_recv.at[k, slot],
            me + 2 * BLOCKS,
        )

    def launch(k):
        hop(k, 0, 1, up).start()
        hop(k, 0, 4, down).start()
        pass_on(k, 0, 0)

    def edge_copy(to):
        return remote(kv.at[0, off], edge, e_send, e_recv, to)

    def send_half():
        @pl.when(ring + 1 < RINGS)
        def _():
            xz(3, me + BLOCKS).start()

        @pl.when(gives_edge)
        def _():
            edge_copy(me + REACH * BLOCKS + 1).start()

    launch(0)

    @pl.when(ring + 4 < RINGS)
    def _():
        xz(2, me + 4 * BLOCKS).start()

    @pl.when(half == 1)
    def _():
        send_half()

    def arrive(k, h):
        @pl.when(from_x(k))
        def _():
            if h == 4:
                x_in(k, 7).wait_recv()
                cross(k, 4, 7).start()
            else:
                x_in(k, h).wait_recv()
                cross(k, -h, h).start()
                x_in(k, 3 + h).wait_recv()
                cross(k, h, 3 + h).start()

        @pl.when(jnp.logical_not(from_x(k)))
        def _():
            if h == 4:
                hop(k, 4, 7, up).wait_recv()
                pass_on(k, 4, 7)
                return
            for side, to, core in ((-1, up, 0), (1, down, 1)):
                slot = h if side < 0 else 3 + h
                hop(k, side * h, slot, to).wait_recv()
                if h < 3:
                    hop(k, side * h, slot + 1, to).start()
                else:

                    @pl.when(c == core)
                    def _():
                        hop(k, side * 3, 7, to).start()

                pass_on(k, side * h, slot)

    lane = lax.broadcasted_iota(jnp.int32, (TOK, TOK), 1)
    row = lax.broadcasted_iota(jnp.int32, (TOK, TOK), 0)
    gap = row - lane

    def fold(blocks, ahead):
        keys = jnp.concatenate([b[pl.ds(0, TOK), :] for b in blocks], axis=0)
        values = jnp.concatenate([b[pl.ds(TOK, TOK), :] for b in blocks], axis=0)
        allowed = []
        for b, a in zip(blocks, ahead):
            seg = b[pl.ds(2 * TOK, 16), :].astype(jnp.float32)[0:1, :]
            allowed.append((seg == qseg[...]) & (gap >= a))
        score = lax.dot_general(
            q[...], keys, (((1,), (1,)), ((), ())), preferred_element_type=jnp.float32
        )
        rounded, keeps = [], []
        for h in range(HEADS):
            parts = [
                jnp.where(
                    allowed[n],
                    score[h * TOK : (h + 1) * TOK, n * TOK : (n + 1) * TOK] * unit_scale,
                    LOW,
                )
                for n in range(len(blocks))
            ]
            old = top[h]
            most = functools.reduce(jnp.maximum, parts)
            new = jnp.maximum(old, jnp.max(most, axis=1, keepdims=True))
            keep = jnp.exp2(old - new)
            weights = [jnp.exp2(p - new) for p in parts]
            top[h] = new
            total[h] = total[h] * keep + functools.reduce(jnp.add, weights)
            rounded.append(jnp.concatenate([w.astype(jnp.bfloat16) for w in weights], axis=1))
            keeps.append(keep)
        product = jnp.dot(
            jnp.concatenate(rounded, axis=0), values, preferred_element_type=jnp.float32
        )
        for h in range(HEADS):
            summed[h] = summed[h] * keeps[h] + product[h * TOK : (h + 1) * TOK]

    def unit(k, h):
        if h < 4:
            cross_in(k, -h, h).wait_recv()
            cross_in(k, h, 3 + h).wait_recv()
            first = (-h, h)
        else:
            cross_in(k, 0, 0).wait_recv()
            cross_in(k, 4, 7).wait_recv()
            first = (0, 4)
        blocks, ahead = [], []
        for dy in first:
            chip = lax.rem(y + dy + RING, RING)
            for core in range(2):
                b = 2 * chip + core
                blocks.append(kv.at[k, b])
                ahead.append((b - off - delta(k) * BLOCKS) * TOK)
        fold(blocks, ahead)

    def drain(k):
        @pl.when(jnp.logical_not(from_x(k)))
        def _():
            for slot in range(1, 8):
                hop(k, 0, slot, up).wait_send()

        @pl.when(feeds_x(k))
        def _():
            for slot in range(8):
                along(k, 0, slot).wait_send()

        for slot in range(8):
            cross(k, 0, slot).wait_send()

    wait = WAIT_LO + (WAIT_HI - WAIT_LO) * half
    last = wait + X_LAG

    def item(place):
        k = jnp.where(place == 0, 0, -1)
        k = jnp.where(place == 1, 2, k)
        k = jnp.where(place == X_LAG, 1, k)
        k = jnp.where(place == wait, 3, k)
        return jnp.where(place == last, 4, k)

    def here(k):
        return (k >= 0) & (ring >= delta(jnp.maximum(k, 0)))

    def begin(k):
        @pl.when(here(k) & from_x(k))
        def _():
            x_in(k, 0).wait_recv()
            cross(k, 0, 0).start()

        @pl.when(here(k) & jnp.logical_not(from_x(k)))
        def _():
            xz(k, me).wait_recv()
            launch(k)

    begin(jnp.int32(2))

    def step(j, _):
        @pl.when((half == 0) & (j == MEET_LO))
        def _():
            pl.semaphore_wait(barrier, others)
            send_half()

        for h in (4, 3, 2, 1):
            now = item(j - LAG * (h - 1))
            past = item(j - LAG * (h - 1) - 1)

            @pl.when(here(now))
            def _():
                arrive(now, h)

            @pl.when(here(past))
            def _():
                unit(past, h)

        begin(item(j + 2))
        done = item(j - LAG * 3 - 1)

        @pl.when(here(done))
        def _():
            drain(done)

        @pl.when(has_edge & (j == last + LAG))
        def _():
            edge_copy(me).wait_recv()
            fold([edge], [jnp.int32(-ITEMS * BLOCKS * TOK + (BLOCKS - 1) * TOK)])

        return 0

    lax.fori_loop(0, last + LAG * 3 + 2, step, 0)

    for h in range(HEADS):
        whole = jnp.sum(total[h], axis=1, keepdims=True)
        o_ref[:, h * HEAD : (h + 1) * HEAD] = (summed[h] * (1.0 / whole)).astype(jnp.bfloat16)

    for k in (2, 3):

        @pl.when(ring + BACK[k] < RINGS)
        def _():
            xz(k, me).wait_send()

    @pl.when(gives_edge)
    def _():
        edge_copy(me).wait_send()


def body(queries, keys, values, segment_ids):
    vmem = pl.BlockSpec(memory_space=pltpu.VMEM)
    return pl.pallas_call(
        kernel,
        out_shape=jax.ShapeDtypeStruct(queries.shape, queries.dtype),
        in_specs=[pl.BlockSpec(memory_space=pltpu.HBM)] * 4,
        out_specs=vmem,
        scratch_shapes=[
            pltpu.VMEM((HEADS * TOK, HEAD), jnp.bfloat16),
            pltpu.VMEM((1, TOK), jnp.int32),
            pltpu.VMEM((ITEMS, BLOCKS, ROWS, HEAD), jnp.bfloat16),
            pltpu.VMEM((ROWS, HEAD), jnp.bfloat16),
            pltpu.VMEM((TOK, TOK), jnp.float32),
            pltpu.VMEM((HEADS, TOK, HEAD), jnp.float32),
            pltpu.VMEM((HEADS, TOK, HEAD), jnp.float32),
            pltpu.VMEM((HEADS, TOK, HEAD), jnp.float32),
            pltpu.SemaphoreType.DMA((3 + HEADS,)),
            pltpu.SemaphoreType.DMA((ITEMS,)),
            pltpu.SemaphoreType.DMA((ITEMS,)),
            pltpu.SemaphoreType.DMA((ITEMS, 8)),
            pltpu.SemaphoreType.DMA((ITEMS, 8)),
            pltpu.SemaphoreType.DMA((ITEMS, 8)),
            pltpu.SemaphoreType.DMA((ITEMS, 8)),
            pltpu.SemaphoreType.DMA((ITEMS, 8)),
            pltpu.SemaphoreType.DMA((ITEMS, 8)),
            pltpu.SemaphoreType.DMA,
            pltpu.SemaphoreType.DMA,
        ],
        compiler_params=pltpu.CompilerParams(
            collective_id=0, has_side_effects=True, vmem_limit_bytes=60 << 20
        ),
        name="attend_ring",
    )(queries, keys, values, segment_ids.reshape(1, TOK))


def solution(mesh):
    return jax.shard_map(
        body,
        mesh=mesh,
        in_specs=(P("ctx", "kvh"), P("ctx", "kvh"), P("ctx", "kvh"), P("ctx")),
        out_specs=P("ctx", "kvh"),
        check_vma=False,
    )
```

time: 69.8 us -> 45.8 us (0.66)
  Pallas kernels: 65.1 us -> 43.6 us
  local copies, waits for them, and re-layouts: 3.73 us -> 1.57 us
    pallas_call x1, Pallas kernels: 65.1 us -> 43.6 us  [body(): pl.pallas_call(kernel, out_shape=jax.ShapeDtypeStruct(queries.shape, quer...]
    unnamed x9 -> x1, local copies, waits for them, and re-layouts: 3.73 us -> 1.57 us
where the time goes in v2:
time: 45.8 us; the launch traced here: 45.2 us
  Pallas kernels  43.6 us (95%)
  local copies, waits for them, and re-layouts  1.57 us (3%)
    pallas_call x1, Pallas kernels, body(): pl.pallas_call(kernel, out_shape=jax.ShapeDtypeStruct(queries.shape, quer...  43.6 us
    unnamed x1, local copies, waits for them, and re-layouts  1.57 us

profile of v2, /device:TPU:7, one launch (start us, length us, event | category | flops | bytes accessed | tf_op | source)
XLA Modules:
  0.0 45.2 jit_solution(11458375649415412766)
XLA Ops:
  0.0 43.6 %attend_ring.1 = bf16[128,512]{1,0:T(8,128)(2,1)} custom-call(bf16[128,512]{1,0:T(8,128)(2,1)} %q_ref.1, bf16[128,128]{1,0:T(8,128)(2,1)} %k_ref.1, bf16[128,128]{1,0:T(8,128)(2,1)} %v_ref.1, s32[1,128]{1,0:T(1,128)} %bitcast.1), custom_call_target="tpu_custom_call" | custom-call | tf_op jit(solution)/shard_map/attend_ring/pallas_call | solution.py:372
  43.6 1.6 %copy.6 = bf16[128,512]{1,0:T(8,128)(2,1)} copy(bf16[128,512]{1,0:T(8,128)(2,1)} %attend_ring.1) | data formatting | bytes 262144

commit v3 on v2

--- a/solution.py
+++ b/solution.py
@@ -19,12 +19,11 @@
 ROWS = 272
 LOW = -2e30
 ITEMS = REACH + 1
+BACK = (0, 2, 4, 1, 3)
+PLACE = {0: 0, 4: 1, -1: 2, 1: 3, -2: 4, 2: 5, -3: 6, 3: 7}
+MEET = 3
+LOW_STEPS, HIGH_STEPS = (0, 3, 1, 5, 8), (0, 3, 1, 4, 7)
 LAG = 2
-BACK = (0, 2, 4, 1, 3)
-MEET_LO = 3
-WAIT_LO, WAIT_HI = 5, 4
-X_LAG = 3
-
 
 def kernel(
     q_ref, k_ref, v_ref, seg_ref, o_ref,
@@ -55,8 +54,8 @@
 
     loads = [
         pltpu.make_async_copy(seg_ref, segs, in_sem.at[0]),
-        pltpu.make_async_copy(k_ref, kv.at[0, off, pl.ds(0, TOK)], in_sem.at[1]),
-        pltpu.make_async_copy(v_ref, kv.at[0, off, pl.ds(TOK, TOK)], in_sem.at[2]),
+        pltpu.make_async_copy(k_ref, kv.at[0, c, 0, pl.ds(0, TOK)], in_sem.at[1]),
+        pltpu.make_async_copy(v_ref, kv.at[0, c, 0, pl.ds(TOK, TOK)], in_sem.at[2]),
     ] + [
         pltpu.make_async_copy(
             q_ref.at[:, pl.ds(h * HEAD, HEAD)], q.at[pl.ds(h * TOK, TOK)], in_sem.at[3 + h]
@@ -109,7 +108,7 @@
     summed[...] = jnp.zeros_like(summed)
     loads[0].wait()
     seg_row = segs[...].astype(jnp.float32)
-    kv[0, off, pl.ds(2 * TOK, 16), :] = jnp.broadcast_to(seg_row, (16, TOK)).astype(jnp.bfloat16)
+    kv[0, c, 0, pl.ds(2 * TOK, 16), :] = jnp.broadcast_to(seg_row, (16, TOK)).astype(jnp.bfloat16)
     qseg[...] = jnp.broadcast_to(seg_row, (TOK, TOK)).T
     for load in loads[1:]:
         load.wait()
@@ -123,53 +122,39 @@
         return lax.rem(2 * k, ITEMS)
 
     def xz(k, to):
-        return remote(kv.at[0, off], kv.at[k, off], xz_send.at[k], xz_recv.at[k], to)
-
-    def hop(k, dy, slot, to):
-        b = at(dy)
-        return remote(kv.at[k, b], kv.at[k, b], y_send.at[k, slot], y_recv.at[k, slot], to)
-
-    def along(k, dy, slot):
-        b = at(dy)
+        return remote(kv.at[0, c, 0], kv.at[k, c, 0], xz_send.at[k], xz_recv.at[k], to)
+
+    def hop(k, here, there, to):
         return remote(
-            kv.at[k, b], kv.at[k + 1, b], x_send.at[k, slot], x_recv.at[k + 1, slot],
-            me + 2 * BLOCKS,
-        )
-
-    def cross(k, dy, slot):
-        b = at(dy)
-        return remote(kv.at[k, b], kv.at[k, b], c_send.at[k, slot], c_recv.at[k, slot], twin)
-
-    def cross_in(k, dy, slot):
-        b = 2 * lax.rem(y + dy + RING, RING) + 1 - c
-        return remote(kv.at[k, b], kv.at[k, b], c_send.at[k, slot], c_recv.at[k, slot], twin)
+            kv.at[k, c, PLACE[here]], kv.at[k, c, PLACE[there]],
+            y_send.at[k], y_recv.at[k, PLACE[there]], to,
+        )
+
+    def pair(h):
+        return pl.ds(2 * (h % 4), 2)
+
+    def along(k, h):
+        return remote(
+            kv.at[k, c, pair(h)], kv.at[k + 1, c, pair(h)],
+            x_send.at[k], x_recv.at[k + 1, h % 4], me + 2 * BLOCKS,
+        )
+
+    def cross(k, h, core):
+        blocks = kv.at[k, core, pair(h)]
+        return remote(blocks, blocks, c_send.at[k], c_recv.at[k, h % 4], twin)
 
     def from_x(k):
-        return (k == 1) | (k == 4)
+        return (k == 1) | ((k == 4) & (c == 0))
 
     def feeds_x(k):
-        return ((k == 0) | (k == 3)) & (ring + 2 < RINGS)
-
-    def pass_on(k, dy, slot):
-        @pl.when(feeds_x(k))
-        def _():
-            along(k, dy, slot).start()
-
-        cross(k, dy, slot).start()
-
-    def x_in(k, slot):
-        return remote(
-            kv.at[k - 1, off], kv.at[k, off], x_send.at[k - 1, slot], x_recv.at[k, slot],
-            me + 2 * BLOCKS,
-        )
+        return ((k == 0) | ((k == 3) & (c == 0))) & (ring + 2 < RINGS)
 
     def launch(k):
-        hop(k, 0, 1, up).start()
-        hop(k, 0, 4, down).start()
-        pass_on(k, 0, 0)
+        hop(k, 0, -1, up).start()
+        hop(k, 0, 1, down).start()
 
     def edge_copy(to):
-        return remote(kv.at[0, off], edge, e_send, e_recv, to)
+        return remote(kv.at[0, c, 0], edge, e_send, e_recv, to)
 
     def send_half():
         @pl.when(ring + 1 < RINGS)
@@ -179,6 +164,10 @@
         @pl.when(gives_edge)
         def _():
             edge_copy(me + REACH * BLOCKS + 1).start()
+
+    @pl.when(half == 1)
+    def _():
+        send_half()
 
     launch(0)
 
@@ -186,40 +175,31 @@
     def _():
         xz(2, me + 4 * BLOCKS).start()
 
-    @pl.when(half == 1)
-    def _():
-        send_half()
-
     def arrive(k, h):
         @pl.when(from_x(k))
         def _():
+            along(k - 1, h).wait_recv()
+
+        @pl.when(jnp.logical_not(from_x(k)))
+        def _():
             if h == 4:
-                x_in(k, 7).wait_recv()
-                cross(k, 4, 7).start()
+                hop(k, 0, 4, up).wait_recv()
             else:
-                x_in(k, h).wait_recv()
-                cross(k, -h, h).start()
-                x_in(k, 3 + h).wait_recv()
-                cross(k, h, 3 + h).start()
-
-        @pl.when(jnp.logical_not(from_x(k)))
-        def _():
-            if h == 4:
-                hop(k, 4, 7, up).wait_recv()
-                pass_on(k, 4, 7)
-                return
-            for side, to, core in ((-1, up, 0), (1, down, 1)):
-                slot = h if side < 0 else 3 + h
-                hop(k, side * h, slot, to).wait_recv()
-                if h < 3:
-                    hop(k, side * h, slot + 1, to).start()
-                else:
-
-                    @pl.when(c == core)
-                    def _():
-                        hop(k, side * 3, 7, to).start()
-
-                pass_on(k, side * h, slot)
+                for side, to, core in ((-1, up, 0), (1, down, 1)):
+                    hop(k, 0, side * h, to).wait_recv()
+                    if h < 3:
+                        hop(k, side * h, side * (h + 1), to).start()
+                    else:
+
+                        @pl.when(c == core)
+                        def _():
+                            hop(k, side * 3, 4, to).start()
+
+        cross(k, h, c).start()
+
+        @pl.when(feeds_x(k))
+        def _():
+            along(k, h).start()
 
     lane = lax.broadcasted_iota(jnp.int32, (TOK, TOK), 1)
     row = lax.broadcasted_iota(jnp.int32, (TOK, TOK), 0)
@@ -261,72 +241,67 @@
             summed[h] = summed[h] * keeps[h] + product[h * TOK : (h + 1) * TOK]
 
     def unit(k, h):
-        if h < 4:
-            cross_in(k, -h, h).wait_recv()
-            cross_in(k, h, 3 + h).wait_recv()
-            first = (-h, h)
-        else:
-            cross_in(k, 0, 0).wait_recv()
-            cross_in(k, 4, 7).wait_recv()
-            first = (0, 4)
+        cross(k, h, 1 - c).wait_recv()
         blocks, ahead = [], []
-        for dy in first:
-            chip = lax.rem(y + dy + RING, RING)
+        for dy in (0, 4) if h == 4 else (-h, h):
             for core in range(2):
-                b = 2 * chip + core
-                blocks.append(kv.at[k, b])
+                b = 2 * lax.rem(y + dy + RING, RING) + core
+                blocks.append(kv.at[k, core, PLACE[dy]])
                 ahead.append((b - off - delta(k) * BLOCKS) * TOK)
         fold(blocks, ahead)
 
     def drain(k):
+        whole = kv.at[k, c]
+
         @pl.when(jnp.logical_not(from_x(k)))
         def _():
-            for slot in range(1, 8):
-                hop(k, 0, slot, up).wait_send()
+            sent = kv.at[k, c, pl.ds(0, 7)]
+            remote(sent, sent, y_send.at[k], y_recv.at[k, 0], up).wait_send()
 
         @pl.when(feeds_x(k))
         def _():
-            for slot in range(8):
-                along(k, 0, slot).wait_send()
-
-        for slot in range(8):
-            cross(k, 0, slot).wait_send()
-
-    wait = WAIT_LO + (WAIT_HI - WAIT_LO) * half
-    last = wait + X_LAG
-
-    def item(place):
-        k = jnp.where(place == 0, 0, -1)
-        k = jnp.where(place == 1, 2, k)
-        k = jnp.where(place == X_LAG, 1, k)
-        k = jnp.where(place == wait, 3, k)
-        return jnp.where(place == last, 4, k)
+            remote(whole, whole, x_send.at[k], x_recv.at[k, 0], twin).wait_send()
+
+        remote(whole, whole, c_send.at[k], c_recv.at[k, 0], twin).wait_send()
+
+    def pick(j):
+        k = jnp.int32(-1)
+        for n, (a, b) in enumerate(zip(LOW_STEPS, HIGH_STEPS)):
+            k = jnp.where(j == a + (b - a) * half, n, k)
+        return k
 
     def here(k):
         return (k >= 0) & (ring >= delta(jnp.maximum(k, 0)))
 
+    def xy():
+        return remote(
+            kv.at[3, c, 0], kv.at[4, c, 0], xz_send.at[4], xz_recv.at[4], me + 2 * BLOCKS
+        )
+
+    hands_on = (c == 1) & (ring >= 1) & (ring + 2 < RINGS)
+
     def begin(k):
-        @pl.when(here(k) & from_x(k))
-        def _():
-            x_in(k, 0).wait_recv()
-            cross(k, 0, 0).start()
-
         @pl.when(here(k) & jnp.logical_not(from_x(k)))
         def _():
             xz(k, me).wait_recv()
+
+            @pl.when((k == 3) & hands_on)
+            def _():
+                xy().start()
+
             launch(k)
 
     begin(jnp.int32(2))
 
     def step(j, _):
-        @pl.when((half == 0) & (j == MEET_LO))
+        @pl.when((half == 0) & (j == MEET))
         def _():
             pl.semaphore_wait(barrier, others)
             send_half()
 
         for h in (4, 3, 2, 1):
-            now = item(j - LAG * (h - 1))
-            past = item(j - LAG * (h - 1) - 1)
+            now = pick(j - LAG * (h - 1))
+            past = pick(j - LAG * (h - 1) - 1)
 
             @pl.when(here(now))
             def _():
@@ -336,21 +311,21 @@
             def _():
                 unit(past, h)
 
-        begin(item(j + 2))
-        done = item(j - LAG * 3 - 1)
+        begin(pick(j + 2))
+        done = pick(j - LAG * 3 - 1)
 
         @pl.when(here(done))
         def _():
             drain(done)
 
-        @pl.when(has_edge & (j == last + LAG))
+        @pl.when(has_edge & (j == LOW_STEPS[4] + LAG))
         def _():
             edge_copy(me).wait_recv()
             fold([edge], [jnp.int32(-ITEMS * BLOCKS * TOK + (BLOCKS - 1) * TOK)])
 
         return 0
 
-    lax.fori_loop(0, last + LAG * 3 + 2, step, 0)
+    lax.fori_loop(0, max(LOW_STEPS[4], HIGH_STEPS[4]) + LAG * 3 + 2, step, 0)
 
     for h in range(HEADS):
         whole = jnp.sum(total[h], axis=1, keepdims=True)
@@ -361,6 +336,10 @@
         @pl.when(ring + BACK[k] < RINGS)
         def _():
             xz(k, me).wait_send()
+
+    @pl.when(hands_on)
+    def _():
+        xy().wait_send()
 
     @pl.when(gives_edge)
     def _():
@@ -377,7 +356,7 @@
         scratch_shapes=[
             pltpu.VMEM((HEADS * TOK, HEAD), jnp.bfloat16),
             pltpu.VMEM((1, TOK), jnp.int32),
-            pltpu.VMEM((ITEMS, BLOCKS, ROWS, HEAD), jnp.bfloat16),
+            pltpu.VMEM((ITEMS, 2, RING, ROWS, HEAD), jnp.bfloat16),
             pltpu.VMEM((ROWS, HEAD), jnp.bfloat16),
             pltpu.VMEM((TOK, TOK), jnp.float32),
             pltpu.VMEM((HEADS, TOK, HEAD), jnp.float32),
@@ -386,12 +365,12 @@
             pltpu.SemaphoreType.DMA((3 + HEADS,)),
             pltpu.SemaphoreType.DMA((ITEMS,)),
             pltpu.SemaphoreType.DMA((ITEMS,)),
-            pltpu.SemaphoreType.DMA((ITEMS, 8)),
-            pltpu.SemaphoreType.DMA((ITEMS, 8)),
-            pltpu.SemaphoreType.DMA((ITEMS, 8)),
-            pltpu.SemaphoreType.DMA((ITEMS, 8)),
-            pltpu.SemaphoreType.DMA((ITEMS, 8)),
-            pltpu.SemaphoreType.DMA((ITEMS, 8)),
+            pltpu.SemaphoreType.DMA((ITEMS,)),
+            pltpu.SemaphoreType.DMA((ITEMS, RING)),
+            pltpu.SemaphoreType.DMA((ITEMS,)),
+            pltpu.SemaphoreType.DMA((ITEMS, 4)),
+            pltpu.SemaphoreType.DMA((ITEMS,)),
+            pltpu.SemaphoreType.DMA((ITEMS, 4)),
             pltpu.SemaphoreType.DMA,
             pltpu.SemaphoreType.DMA,
         ],

time: 45.8 us -> 44 us (0.961)
  Pallas kernels: 43.6 us -> 42 us
    pallas_call x1, Pallas kernels: 43.6 us -> 42 us  [body(): pl.pallas_call(kernel, out_shape=jax.ShapeDtypeStruct(queries.shape, quer...]
where the time goes in v3:
time: 44 us; the launch traced here: 43.6 us
  Pallas kernels  42 us (95%)
  local copies, waits for them, and re-layouts  1.57 us (4%)
    pallas_call x1, Pallas kernels, body(): pl.pallas_call(kernel, out_shape=jax.ShapeDtypeStruct(queries.shape, quer...  42 us
    unnamed x1, local copies, waits for them, and re-layouts  1.57 us

profile of v3, /device:TPU:7, one launch (start us, length us, event | category | flops | bytes accessed | tf_op | source)
XLA Modules:
  0.0 43.6 jit_solution(10036136084247491089)
XLA Ops:
  0.0 42.0 %attend_ring.1 = bf16[128,512]{1,0:T(8,128)(2,1)} custom-call(bf16[128,512]{1,0:T(8,128)(2,1)} %q_ref.1, bf16[128,128]{1,0:T(8,128)(2,1)} %k_ref.1, bf16[128,128]{1,0:T(8,128)(2,1)} %v_ref.1, s32[1,128]{1,0:T(1,128)} %bitcast.1), custom_call_target="tpu_custom_call" | custom-call | tf_op jit(solution)/shard_map/attend_ring/pallas_call | solution.py:351
  42.0 1.6 %copy.6 = bf16[128,512]{1,0:T(8,128)(2,1)} copy(bf16[128,512]{1,0:T(8,128)(2,1)} %attend_ring.1) | data formatting | bytes 262144

commit v4 on v3

--- a/solution.py
+++ b/solution.py
@@ -21,14 +21,14 @@
 ITEMS = REACH + 1
 BACK = (0, 2, 4, 1, 3)
 PLACE = {0: 0, 4: 1, -1: 2, 1: 3, -2: 4, 2: 5, -3: 6, 3: 7}
-MEET = 3
+MEET = 2
 LOW_STEPS, HIGH_STEPS = (0, 3, 1, 5, 8), (0, 3, 1, 4, 7)
 LAG = 2
 
 def kernel(
     q_ref, k_ref, v_ref, seg_ref, o_ref,
     q, segs, kv, edge, qseg, top, total, summed, in_sem,
-    xz_send, xz_recv, y_send, y_recv, x_send, x_recv, c_send, c_recv, e_send, e_recv,
+    xz_send, xz_recv, y_send, y_recv, x_send, x_recv, c_send, c_recv, t_send, e_send, e_recv,
 ):
     me = lax.axis_index("ctx")
     off = lax.rem(me, BLOCKS)
@@ -64,6 +64,8 @@
     ]
     for load in loads:
         load.start()
+
+    kv[2] = jnp.zeros(kv.shape[1:], kv.dtype)
 
     has_edge = (off == 0) & (ring >= ITEMS)
     gives_edge = (off == BLOCKS - 1) & (ring + ITEMS < RINGS)
@@ -130,6 +132,67 @@
             y_send.at[k], y_recv.at[k, PLACE[there]], to,
         )
 
+    def trim(here, there, to, n):
+        return remote(
+            kv.at[2, c, PLACE[here]], kv.at[2, c, PLACE[there]],
+            t_send.at[n], y_recv.at[2, PLACE[there]], to,
+        )
+
+    def source(h):
+        return lax.rem(y - h + RING, RING)
+
+    def trims():
+        out = []
+        for h in range(3):
+            go = source(h) >= 5
+            if h == 0:
+                go = go | (c == 1)
+            out.append((go, functools.partial(trim, -h, -h - 1, up, h)))
+        for h in range(4):
+            out.append(((y + h < RING) & (y >= 1), functools.partial(trim, h, h + 1, down, 3 + h)))
+        return out
+
+    def start_trim(n):
+        go, copy = trims()[n]
+
+        @pl.when(go)
+        def _():
+            copy().start()
+
+    def arrive_trim(h):
+        if h == 4:
+
+            @pl.when(y < 4)
+            def _():
+                hop(2, 0, 4, down).wait_recv()
+
+            return
+        comes = source(h) >= 5
+        if h == 1:
+            comes = comes | (c == 1)
+
+        @pl.when(comes)
+        def _():
+            hop(2, 0, -h, up).wait_recv()
+
+        if h < 3:
+            start_trim(h)
+
+        @pl.when(y + h < RING)
+        def _():
+            hop(2, 0, h, down).wait_recv()
+
+        start_trim(3 + h)
+
+    def absent(dy, core):
+        if dy == 0:
+            return jnp.bool_(False)
+        if dy > 0:
+            return y + dy >= RING
+        if dy == -1 and core == 1:
+            return jnp.bool_(False)
+        return y + dy >= 0
+
     def pair(h):
         return pl.ds(2 * (h % 4), 2)
 
@@ -150,8 +213,15 @@
         return ((k == 0) | ((k == 3) & (c == 0))) & (ring + 2 < RINGS)
 
     def launch(k):
-        hop(k, 0, -1, up).start()
-        hop(k, 0, 1, down).start()
+        @pl.when(k == 2)
+        def _():
+            start_trim(0)
+            start_trim(3)
+
+        @pl.when(k != 2)
+        def _():
+            hop(k, 0, -1, up).start()
+            hop(k, 0, 1, down).start()
 
     def edge_copy(to):
         return remote(kv.at[0, c, 0], edge, e_send, e_recv, to)
@@ -180,7 +250,11 @@
         def _():
             along(k - 1, h).wait_recv()
 
-        @pl.when(jnp.logical_not(from_x(k)))
+        @pl.when(k == 2)
+        def _():
+            arrive_trim(h)
+
+        @pl.when(jnp.logical_not(from_x(k)) & (k != 2))
         def _():
             if h == 4:
                 hop(k, 0, 4, up).wait_recv()
@@ -247,13 +321,22 @@
             for core in range(2):
                 b = 2 * lax.rem(y + dy + RING, RING) + core
                 blocks.append(kv.at[k, core, PLACE[dy]])
-                ahead.append((b - off - delta(k) * BLOCKS) * TOK)
+                a = (b - off - delta(k) * BLOCKS) * TOK
+                ahead.append(jnp.where((k == 2) & absent(dy, core), TOK, a))
         fold(blocks, ahead)
 
     def drain(k):
         whole = kv.at[k, c]
 
-        @pl.when(jnp.logical_not(from_x(k)))
+        @pl.when(k == 2)
+        def _():
+            for go, copy in trims():
+
+                @pl.when(go)
+                def _():
+                    copy().wait_send()
+
+        @pl.when(jnp.logical_not(from_x(k)) & (k != 2))
         def _():
             sent = kv.at[k, c, pl.ds(0, 7)]
             remote(sent, sent, y_send.at[k], y_recv.at[k, 0], up).wait_send()
@@ -301,7 +384,7 @@
 
         for h in (4, 3, 2, 1):
             now = pick(j - LAG * (h - 1))
-            past = pick(j - LAG * (h - 1) - 1)
+            past = pick(j - LAG * (h - 1) - 2)
 
             @pl.when(here(now))
             def _():
@@ -325,7 +408,7 @@
 
         return 0
 
-    lax.fori_loop(0, max(LOW_STEPS[4], HIGH_STEPS[4]) + LAG * 3 + 2, step, 0)
+    lax.fori_loop(0, max(LOW_STEPS[4], HIGH_STEPS[4]) + LAG * 3 + 3, step, 0)
 
     for h in range(HEADS):
         whole = jnp.sum(total[h], axis=1, keepdims=True)
@@ -371,6 +454,7 @@
             pltpu.SemaphoreType.DMA((ITEMS, 4)),
             pltpu.SemaphoreType.DMA((ITEMS,)),
             pltpu.SemaphoreType.DMA((ITEMS, 4)),
+            pltpu.SemaphoreType.DMA((7,)),
             pltpu.SemaphoreType.DMA,
             pltpu.SemaphoreType.DMA,
         ],

time: 44 us -> 43.5 us (0.989)
  no operation moved by 1% of the time
where the time goes in v4:
time: 43.5 us; the launch traced here: 43.3 us
  Pallas kernels  41.7 us (96%)
  local copies, waits for them, and re-layouts  1.57 us (4%)
    pallas_call x1, Pallas kernels, body(): pl.pallas_call(kernel, out_shape=jax.ShapeDtypeStruct(queries.shape, quer...  41.7 us
    unnamed x1, local copies, waits for them, and re-layouts  1.57 us

profile of v4, /device:TPU:7, one launch (start us, length us, event | category | flops | bytes accessed | tf_op | source)
XLA Modules:
  0.0 43.3 jit_solution(15724044063911432676)
XLA Ops:
  0.0 41.7 %attend_ring.1 = bf16[128,512]{1,0:T(8,128)(2,1)} custom-call(bf16[128,512]{1,0:T(8,128)(2,1)} %q_ref.1, bf16[128,128]{1,0:T(8,128)(2,1)} %k_ref.1, bf16[128,128]{1,0:T(8,128)(2,1)} %v_ref.1, s32[1,128]{1,0:T(1,128)} %bitcast.1), custom_call_target="tpu_custom_call" | custom-call | tf_op jit(solution)/shard_map/attend_ring/pallas_call | solution.py:434
  41.7 1.6 %copy.6 = bf16[128,512]{1,0:T(8,128)(2,1)} copy(bf16[128,512]{1,0:T(8,128)(2,1)} %attend_ring.1) | data formatting | bytes 262144

commit v5 on v4

--- a/solution.py
+++ b/solution.py
@@ -22,7 +22,7 @@
 BACK = (0, 2, 4, 1, 3)
 PLACE = {0: 0, 4: 1, -1: 2, 1: 3, -2: 4, 2: 5, -3: 6, 3: 7}
 MEET = 2
-LOW_STEPS, HIGH_STEPS = (0, 3, 1, 5, 8), (0, 3, 1, 4, 7)
+LOW_STEPS, HIGH_STEPS = (0, 3, 1, 4, 7), (0, 3, 1, 4, 7)
 LAG = 2
 
 def kernel(

time: 43.5 us -> 42.6 us (0.979)
  the two profiles are of different devices: /device:TPU:7 before, /device:TPU:5 now
where the time goes in v5:
time: 42.6 us; the launch traced here: 42.4 us
  Pallas kernels  40.9 us (96%)
  local copies, waits for them, and re-layouts  1.57 us (4%)
    pallas_call x1, Pallas kernels, body(): pl.pallas_call(kernel, out_shape=jax.ShapeDtypeStruct(queries.shape, quer...  40.9 us
    unnamed x1, local copies, waits for them, and re-layouts  1.57 us

profile of v5, /device:TPU:5, one launch (start us, length us, event | category | flops | bytes accessed | tf_op | source)
XLA Modules:
  0.0 42.4 jit_solution(15792946560681319292)
XLA Ops:
  0.0 40.9 %attend_ring.1 = bf16[128,512]{1,0:T(8,128)(2,1)} custom-call(bf16[128,512]{1,0:T(8,128)(2,1)} %q_ref.1, bf16[128,128]{1,0:T(8,128)(2,1)} %k_ref.1, bf16[128,128]{1,0:T(8,128)(2,1)} %v_ref.1, s32[1,128]{1,0:T(1,128)} %bitcast.1), custom_call_target="tpu_custom_call" | custom-call | tf_op jit(solution)/shard_map/attend_ring/pallas_call | solution.py:434
  40.9 1.6 %copy.6 = bf16[128,512]{1,0:T(8,128)(2,1)} copy(bf16[128,512]{1,0:T(8,128)(2,1)} %attend_ring.1) | data formatting | bytes 262144
